TPU v7x, 32 devices: a whole 2x2x4 slice. The times are simulated.
32 devices in a mesh: groups: 2 (over x), seq: 16 (over z, y, core).
Axes of the slice: x: 2, y: 2, z: 4, core: 2. Of those that a mesh axis runs over, the one named last changes fastest.
Arguments:
- query: bfloat16 [8192, 1536], P(('groups', 'seq')), parts along dimension 0, may hold values from -6 to 6
- keys: bfloat16 [8192, 1536], P(('groups', 'seq')), parts along dimension 0, may hold values from -6 to 6
- values: bfloat16 [8192, 1536], P(('groups', 'seq')), parts along dimension 0, may hold values from -6 to 6
- allowed: int32 [64, 4], P(('groups', 'seq')), parts along dimension 0, may hold values from -1 to 31, as said below
- kernel: float32 [31, 1536], replicated, may hold values from -4 to 4
- cotangent: bfloat16 [8192, 1536], P(('groups', 'seq')), parts along dimension 0, may hold values from -6 to 6
Outputs:
- conv_out: bfloat16 [8192, 1536], P(('groups', 'seq')), parts along dimension 0
- query_grad: bfloat16 [8192, 1536], P(('groups', 'seq')), parts along dimension 0
- keys_grad: bfloat16 [8192, 1536], P(('groups', 'seq')), parts along dimension 0
- values_grad: bfloat16 [8192, 1536], P(('groups', 'seq')), parts along dimension 0
- kernel_grad: float32 [62, 1536], P('groups'), parts along dimension 0
There are 2 independent parts, one for each index of `groups`. A program takes and returns all parts, laid end to end along the dimension named above; an argument that names none is the same for every part. Nothing has to cross between parts.
Inputs may be any that keep to these rules, and one draw needn't show every extreme that they name: `allowed`: row b lists b first, then three distinct earlier blocks between b - 8 and b - 1, or -1 where such a block would lie before frame 0; the last row reaches back exactly 8 blocks.
All inputs are finite; a program needn't handle non-finite values.
Results may differ from a plain program's by a relative error of at most 0.012.
Values may be sent and summed in bfloat16 or wider, within the bound.
A program may use at most 128 MiB of HBM per device.

v0:
```python
import jax
import jax.numpy as jnp
from jax import lax
from jax.sharding import PartitionSpec as P

HD = 64
KERNEL = 31
BLOCK = 128
SPAN_DEV = 4
SCALE = 0.125
NEG = -1e30


def shifted(block, axis, distance):
    devices = range(lax.axis_size(axis))
    route = [(i - distance, i) for i in devices if i - distance in devices]
    return lax.ppermute(block, axis, route)


def with_halo(block, sides, width):
    for axis, dim in sides:
        count = lax.axis_size(axis)
        forward = [(i, i + 1) for i in range(count - 1)]
        backward = [(target, source) for source, target in forward]
        low = lax.ppermute(
            lax.slice_in_dim(block, block.shape[dim] - width, None, axis=dim), axis, forward
        )
        high = lax.ppermute(lax.slice_in_dim(block, 0, width, axis=dim), axis, backward)
        block = jnp.concatenate([low, block, high], axis=dim)
    return block


def head_major(matrix, heads):
    return matrix.reshape(matrix.shape[0], heads, HD).transpose(1, 0, 2)


def row_major(array):
    return array.transpose(1, 0, 2).reshape(array.shape[1], array.shape[0] * array.shape[2])


def attend(query_head, key_head, frame_ok):
    scores = jnp.dot(query_head, key_head.T, preferred_element_type=jnp.float32) * SCALE
    scores = jnp.where(frame_ok, scores, NEG)
    peak = jnp.max(scores, axis=-1, keepdims=True)
    expo = jnp.exp(scores - peak)
    total = jnp.sum(expo, axis=-1, keepdims=True)
    return (expo / total, peak[:, 0] + jnp.log(total[:, 0]))


def local(query, keys, values, allowed, kernel, cotangent):
    frames, width = query.shape
    heads = width // HD
    blocks_dev = frames // BLOCK
    half = KERNEL // 2
    own_index = lax.axis_index("seq")
    stacked = jnp.stack([keys, values])
    pieces = [stacked]
    carried = stacked
    for distance in range(1, SPAN_DEV + 1):
        carried = shifted(carried, "seq", 1)
        pieces.append(carried)
    candidates = jnp.concatenate(pieces, axis=1)
    key_ids = jnp.concatenate(
        [
            own_index * blocks_dev - distance * blocks_dev + jnp.arange(blocks_dev, dtype=jnp.int32)
            for distance in range(SPAN_DEV + 1)
        ]
    )
    block_ok = (
        jnp.any(allowed[:, :, None] == key_ids[None, None, :], axis=1) & (key_ids >= 0)[None, :]
    )
    frame_ok = jnp.repeat(jnp.repeat(block_ok, BLOCK, axis=0), BLOCK, axis=1)
    query_heads = head_major(query, heads)
    key_heads = head_major(candidates[0], heads)
    value_heads = head_major(candidates[1], heads)

    def forward_head(inputs):
        query_head, key_head, value_head = inputs
        probs, log_total = attend(query_head, key_head, frame_ok)
        return (
            jnp.dot(probs.astype(jnp.bfloat16), value_head, preferred_element_type=jnp.float32),
            log_total,
        )

    attended_heads, log_totals = lax.map(forward_head, (query_heads, key_heads, value_heads))
    attended = row_major(attended_heads)
    attended_half = attended.astype(jnp.bfloat16)
    padded = with_halo(attended_half, (("seq", 0),), KERNEL // 2)
    cot_pad = with_halo(cotangent, (("seq", 0),), KERNEL // 2)
    cot_float = cotangent.astype(jnp.float32)
    conv_sum = jnp.zeros((frames, width), jnp.float32)
    grad_sum = jnp.zeros((frames, width), jnp.float32)
    taps_grad = []
    for offset in range(KERNEL):
        window = padded[offset : offset + frames].astype(jnp.float32)
        conv_sum = conv_sum + kernel[offset][None, :] * window
        grad_sum = grad_sum + kernel[offset][None, :] * cot_pad[
            2 * half - offset : 2 * half - offset + frames
        ].astype(jnp.float32)
        taps_grad.append(jnp.sum(cot_float * window, axis=0))
    conv_out = conv_sum.astype(jnp.bfloat16)
    attended_grad = grad_sum.astype(jnp.bfloat16)
    kernel_grad = lax.psum(jnp.stack(taps_grad), "seq")
    grad_heads = head_major(attended_grad, heads)
    out_heads = head_major(attended, heads)
    deltas = jnp.sum(grad_heads.astype(jnp.float32) * out_heads, axis=-1)

    def backward_head(inputs):
        query_head, key_head, value_head, grad_head, delta_head = inputs
        probs, unused = attend(query_head, key_head, frame_ok)
        probs_half = probs.astype(jnp.bfloat16)
        probs_grad = jnp.dot(grad_head, value_head.T, preferred_element_type=jnp.float32)
        scores_grad = (SCALE * probs * (probs_grad - delta_head[:, None])).astype(jnp.bfloat16)
        query_part = jnp.dot(scores_grad, key_head, preferred_element_type=jnp.float32)
        keys_part = jnp.einsum(
            "qk,qd->kd", scores_grad, query_head, preferred_element_type=jnp.float32
        )
        values_part = jnp.einsum(
            "qk,qd->kd", probs_half, grad_head, preferred_element_type=jnp.float32
        )
        return (query_part, keys_part, values_part)

    query_part, keys_part, values_part = lax.map(
        backward_head, (query_heads, key_heads, value_heads, grad_heads, deltas)
    )
    query_grad = row_major(query_part).astype(jnp.bfloat16)
    grads = jnp.stack([row_major(keys_part), row_major(values_part)])
    terms = [
        grads[:, distance * frames : (distance + 1) * frames] for distance in range(SPAN_DEV + 1)
    ]
    totals = terms[SPAN_DEV]
    for distance in range(SPAN_DEV - 1, -1, -1):
        totals = (
            shifted(totals.astype(jnp.bfloat16), "seq", -1).astype(totals.dtype) + terms[distance]
        )
    keys_total = totals[0]
    values_total = totals[1]
    keys_grad = keys_total.astype(jnp.bfloat16)
    values_grad = values_total.astype(jnp.bfloat16)
    return (conv_out, query_grad, keys_grad, values_grad, kernel_grad)


def solution(mesh):
    placed = (
        P(("groups", "seq"), None),
        P(("groups", "seq"), None),
        P(("groups", "seq"), None),
        P(("groups", "seq"), None),
        P(),
        P(("groups", "seq"), None),
    )
    return jax.shard_map(
        local,
        mesh=mesh,
        in_specs=placed,
        out_specs=(
            P(("groups", "seq"), None),
            P(("groups", "seq"), None),
            P(("groups", "seq"), None),
            P(("groups", "seq"), None),
            P("groups", None),
        ),
        check_vma=False,
    )
```

profile of v0, /device:TPU:0, one launch (start us, length us, event | category | flops | bytes accessed | tf_op | source)
XLA Modules:
  0.0 679.3 jit_solution(14867233980165950894)
XLA Ops:
  10.4 2.4 collective-permute-start
  12.9 2.9 collective-permute-done
  17.0 20.1 %collective-permute-start.1 = (bf16[2,256,1536]{1,2,0:T(8,128)(2,1)S(1)}, bf16[2,256,1536]{1,2,0:T(8,128)(2,1)}, u32[]{:S(2)}, u32[]{:S(2)}) collective-permute-start(bf16[2,256,1536]{1,2,0:T(8,128)(2,1)S(1)} %collective-permute-done), channel_id=1, source_target_pairs={{0,1},{1,2},{2,3},{3,4},{4,5},{5,6},{6,7},{7,8},{8,9},{9,10},{10,1... | collective-permute-start | bytes 4718600 | tf_op jit(solution)/shard_map/ppermute | solution.py:17
  39.0 19.7 %collective-permute-start.2 = (bf16[2,256,1536]{1,2,0:T(8,128)(2,1)}, bf16[2,256,1536]{1,2,0:T(8,128)(2,1)}, u32[]{:S(2)}, u32[]{:S(2)}) collective-permute-start(bf16[2,256,1536]{1,2,0:T(8,128)(2,1)} %collective-permute-done.1), channel_id=1, source_target_pairs={{0,1},{1,2},{2,3},{3,4},{4,5},{5,6},{6,7},{7,8},{8,9},{9,10},{10,1... | collective-permute-start | bytes 4718600 | tf_op jit(solution)/shard_map/ppermute | solution.py:17
  59.7 3.4 collective-permute-start.7
  65.7 2.1 slice_reduce_fusion.29
  67.8 2.5 slice_reduce_fusion.30
  72.8 11.2 %collective-permute-start.3 = (bf16[2,256,1536]{1,2,0:T(8,128)(2,1)}, bf16[2,256,1536]{1,2,0:T(8,128)(2,1)S(1)}, u32[]{:S(2)}, u32[]{:S(2)}) collective-permute-start(bf16[2,256,1536]{1,2,0:T(8,128)(2,1)} %collective-permute-done.2), channel_id=1, source_target_pairs={{0,1},{1,2},{2,3},{3,4},{4,5},{5,6},{6,7},{7,8},{8,9},{9,10},{10,1... | collective-permute-start | bytes 4718600 | tf_op jit(solution)/shard_map/ppermute | solution.py:17
  84.0 27.4 %fusion.136 = bf16[256,1536]{0,1:T(8,128)(2,1)} fusion(bf16[256,1536]{0,1:T(8,128)(2,1)S(1)} %copy.71, bf16[15,1536]{0,1:T(8,128)(2,1)S(1)} %collective-permute-done.7, bf16[15,1536]{0,1:T(8,128)(2,1)} %collective-permute-done.6, f32[1536]{0:T(1024)} %get-tuple-element.256, f32[1536]{0:T(1024)} %get-tuple-element.257, f32[1536]{0:T(1024)} %get-tuple-element.228, ...), kind=kLoop, calls=%fused_computation.330 | loop fusion | flops 71958528 | bytes 1855488 | tf_op jit(solution)/shard_map/convert_element_type | solution.py:102
  112.8 2.7 constant_dynamic-update-slice_fusion.2
  115.5 2.8 constant_dynamic-update-slice_fusion.1
  119.7 5.6 fusion.195
  125.2 8.3 %copy.68 = bf16[24,1280,64]{2,1,0:T(8,128)(2,1)} copy(bf16[24,1280,64]{1,2,0:T(8,128)(2,1)} %bitcast.179) | data formatting | bytes 7864320
  133.5 8.2 %copy.69 = bf16[24,1280,64]{2,1,0:T(8,128)(2,1)} copy(bf16[24,1280,64]{1,2,0:T(8,128)(2,1)} %bitcast.178) | data formatting | bytes 7864320
  141.7 104.6 %while.28 = (s32[]{:T(128)}, f32[24,256,64]{1,2,0:T(8,128)}, bf16[24,256,64]{2,1,0:T(8,128)(2,1)S(1)}, bf16[24,1280,64]{2,1,0:T(8,128)(2,1)}, bf16[24,1280,64]{2,1,0:T(8,128)(2,1)}, /*index=5*/pred[256,10]{0,1:T(8,128)(4,1)S(1)}) while((s32[]{:T(128)}, f32[24,256,64]{1,2,0:T(8,128)}, ...), condition=%wide.region_4.5_spmd.clone.clone, body=%wide.region_1.4_spmd.clone.sunk.clone | while | flops 86507008 | bytes 6039117 | solution.py:85
  152.7 2.1 fusion.239
  157.1 2.1 fusion.239
  170.1 2.1 fusion.239
  174.5 2.1 fusion.239
  178.9 2.1 fusion.239
  183.2 2.1 fusion.239
  187.6 2.1 fusion.239
  191.9 2.1 fusion.239
  196.3 2.1 fusion.239
  200.7 2.1 fusion.239
  205.0 2.1 fusion.239
  213.7 2.1 fusion.239
  222.4 2.1 fusion.239
  226.8 2.1 fusion.239
  231.2 2.1 fusion.239
  239.9 2.1 fusion.239
  244.2 2.1 fusion.239
  246.3 2.5 multiply_reduce_fusion
  248.8 208.7 %while.29 = (s32[]{:T(128)}, bf16[24,256,64]{1,2,0:T(8,128)(2,1)}, f32[24,1280,64]{1,2,0:T(8,128)}, f32[24,1280,64]{1,2,0:T(8,128)}, bf16[24,256,64]{2,1,0:T(8,1...) while((s32[]{:T(128)}, bf16[24,256,64]{1,2,0:T(8,128)(2,1)}, ...), condition=%wide.region_9.10_spmd.clone.clone, body=%wide.region_6.9_spmd.clone.sunk.clone | while | flops 214302208 | bytes 10438257 | solution.py:123
  457.5 2.3 fusion.49
  461.4 6.0 collective-permute-done.8
  471.4 20.0 %collective-permute-start.4 = (bf16[15,1536]{0,1:T(8,128)(2,1)}, bf16[15,1536]{0,1:T(8,128)(2,1)S(1)}, u32[]{:S(2)}, u32[]{:S(2)}) collective-permute-start(bf16[15,1536]{0,1:T(8,128)(2,1)} %bitcast.9), channel_id=1, source_target_pairs={{0,1},{1,2},{2,3},{3,4},{4,5},{5,6},{6,7},{7,8},{8,9},{9,10},{10,1... | collective-permute-start | bytes 138248 | tf_op jit(solution)/shard_map/ppermute | solution.py:25
  494.0 5.7 fusion.119
  500.0 2.9 fusion.55
  504.6 19.3 %fusion.88 = bf16[256,1536]{0,1:T(8,128)(2,1)S(1)} fusion(bf16[256,1536]{0,1:T(8,128)(2,1)S(1)} %bitcast.172, f32[1536]{0:T(1024)S(1)} %copy-done.35, f32[1536]{0:T(1024)S(1)} %copy-done.36, f32[1536]{0:T(1024)S(1)} %copy-done.7, f32[1536]{0:T(1024)S(1)} %copy-done.8, f32[1536]{0:T(1024)S(1)} %copy-done.9, f32[1536]{0:T(1024)S(1)} %copy-done.10, ...), kind=kLoop, calls=%fused_computation.280 | loop fusion | flops 71958528 | bytes 1855488 | tf_op jit(solution)/shard_map/convert_element_type | solution.py:101
  523.9 4.6 collective-permute-done.10
  531.4 3.7 fusion.118
  536.4 6.0 fusion.135
  542.4 4.4 fusion.134
  547.0 2.8 stack.143
  549.8 3.0 collective-permute-done.11
  552.8 2.7 fusion.57
  557.9 112.9 %all-reduce.2.cloned.1.call-done = f32[31,1536]{1,0:T(8,128)} async-done(((f32[31,1536]{1,0:T(8,128)}), f32[31,1536]{1,0:T(8,128)}) %all-reduce.2.cloned.1.call-update) | async-done | bytes 190480 | tf_op jit(solution)/shard_map/psum | solution.py:103
  (492 shorter events, 310.2 us)
Async XLA Ops:
  7.2 663.7 %all-reduce.2.cloned.1.call-start = ((), (), s32[]{:S(2)}) async-start(), calls=%async_computation | async-start | bytes 393216 | tf_op jit(solution)/shard_map/psum | solution.py:103
  9.0 49.7 %copy-start.4 = (bf16[256,1536]{1,0:T(8,128)(2,1)S(1)}, bf16[256,1536]{1,0:T(8,128)(2,1)}, u32[]{:S(2)}) copy-start(bf16[256,1536]{1,0:T(8,128)(2,1)} %param.15) | copy-start | bytes 2359300
  9.0 56.5 %copy-start.37 = (s32[2,4]{1,0:T(2,128)S(1)}, s32[2,4]{1,0:T(2,128)}, u32[]{:S(2)}) copy-start(s32[2,4]{1,0:T(2,128)} %param.13) | copy-start | bytes 100
  10.4 5.4 collective-permute-start
  17.0 22.0 %collective-permute-start.1 = (bf16[2,256,1536]{1,2,0:T(8,128)(2,1)S(1)}, bf16[2,256,1536]{1,2,0:T(8,128)(2,1)}, u32[]{:S(2)}, u32[]{:S(2)}) collective-permute-start(bf16[2,256,1536]{1,2,0:T(8,128)(2,1)S(1)} %collective-permute-done), channel_id=1, source_target_pairs={{0,1},{1,2},{2,3},{3,4},{4,5},{5,6},{6,7},{7,8},{8,9},{9,10},{10,1... | collective-permute-start | bytes 4718600 | tf_op jit(solution)/shard_map/ppermute | solution.py:17
  39.0 33.9 %collective-permute-start.2 = (bf16[2,256,1536]{1,2,0:T(8,128)(2,1)}, bf16[2,256,1536]{1,2,0:T(8,128)(2,1)}, u32[]{:S(2)}, u32[]{:S(2)}) collective-permute-start(bf16[2,256,1536]{1,2,0:T(8,128)(2,1)} %collective-permute-done.1), channel_id=1, source_target_pairs={{0,1},{1,2},{2,3},{3,4},{4,5},{5,6},{6,7},{7,8},{8,9},{9,10},{10,1... | collective-permute-start | bytes 4718600 | tf_op jit(solution)/shard_map/ppermute | solution.py:17
  59.7 24.3 %collective-permute-start.7 = (bf16[15,1536]{0,1:T(8,128)(2,1)}, bf16[15,1536]{0,1:T(8,128)(2,1)S(1)}, u32[]{:S(2)}, u32[]{:S(2)}) collective-permute-start(bf16[15,1536]{0,1:T(8,128)(2,1)} %copy.73), channel_id=1, source_target_pairs={{0,1},{1,2},{2,3},{3,4},{4,5},{5,6},{6,7},{7,8},{8,9},{9,10},{10,1... | collective-permute-start | bytes 138248 | tf_op jit(solution)/shard_map/ppermute | solution.py:25
  63.1 8.6 %copy-start.6 = (bf16[256,1536]{1,0:T(8,128)(2,1)S(1)}, bf16[256,1536]{1,0:T(8,128)(2,1)}, u32[]{:S(2)}) copy-start(bf16[256,1536]{1,0:T(8,128)(2,1)} %param.10) | copy-start | bytes 2359300
  64.0 20.0 %collective-permute-start.6 = (bf16[15,1536]{0,1:T(8,128)(2,1)}, bf16[15,1536]{0,1:T(8,128)(2,1)}, u32[]{:S(2)}, u32[]{:S(2)}) collective-permute-start(bf16[15,1536]{0,1:T(8,128)(2,1)} %copy.70), channel_id=1, source_target_pairs={{1,0},{2,1},{3,2},{4,3},{5,4},{6,5},{7,6},{8,7},{9,8},{10,9},{11,1... | collective-permute-start | bytes 138248 | tf_op jit(solution)/shard_map/ppermute | solution.py:28
  72.8 38.6 %copy-start.3 = (bf16[2,256,1536]{1,2,0:T(8,128)(2,1)S(1)}, bf16[2,256,1536]{1,2,0:T(8,128)(2,1)}, u32[]{:S(2)}) copy-start(bf16[2,256,1536]{1,2,0:T(8,128)(2,1)} %copy-done.2) | copy-start | bytes 4718596
  72.8 45.5 %collective-permute-start.3 = (bf16[2,256,1536]{1,2,0:T(8,128)(2,1)}, bf16[2,256,1536]{1,2,0:T(8,128)(2,1)S(1)}, u32[]{:S(2)}, u32[]{:S(2)}) collective-permute-start(bf16[2,256,1536]{1,2,0:T(8,128)(2,1)} %collective-permute-done.2), channel_id=1, source_target_pairs={{0,1},{1,2},{2,3},{3,4},{4,5},{5,6},{6,7},{7,8},{8,9},{9,10},{10,1... | collective-permute-start | bytes 4718600 | tf_op jit(solution)/shard_map/ppermute | solution.py:17
  457.5 9.9 %slice-start = ((s8[7864320]{0:T(1024)(128)(4,1)}), s8[4194304]{0:T(1024)(128)(4,1)S(1)}, s32[]{:S(2)}) async-start(s8[7864320]{0:T(1024)(128)(4,1)} %bitcast.157), calls=%async_computation.1 | async-start | bytes 8388608
  457.5 9.9 %slice-start.1 = ((s8[7864320]{0:T(1024)(128)(4,1)}), s8[3670016]{0:T(1024)(128)(4,1)S(1)}, s32[]{:S(2)}) async-start(s8[7864320]{0:T(1024)(128)(4,1)} %bitcast.157), calls=%async_computation.2 | async-start | bytes 7340032
  457.5 9.9 %copy-start = (f32[24,1280,64]{1,2,0:T(8,128)S(1)}, f32[24,1280,64]{1,2,0:T(8,128)}, u32[]{:S(2)}) copy-start(f32[24,1280,64]{1,2,0:T(8,128)} %get-tuple-element.93) | copy-start | bytes 23592964
  459.8 7.6 %collective-permute-start.8 = (bf16[2,256,1536]{1,2,0:T(8,128)(2,1)S(1)}, bf16[2,256,1536]{1,2,0:T(8,128)(2,1)S(1)}, u32[]{:S(2)}, u32[]{:S(2)}) collective-permute-start(bf16[2,256,1536]{1,2,0:T(8,128)(2,1)S(1)} %fusion.49), channel_id=1, source_target_pairs={{1,0},{2,1},{3,2},{4,3},{5,4},{6,5},{7,6},{8,7},{9,8},{10,9},{11,1... | collective-permute-start | bytes 4718600 | tf_op jit(solution)/shard_map/ppermute | solution.py:17
  469.1 22.4 %copy-start.1 = (bf16[24,256,64]{1,2,0:T(8,128)(2,1)S(1)}, bf16[24,256,64]{1,2,0:T(8,128)(2,1)}, u32[]{:S(2)}) copy-start(bf16[24,256,64]{1,2,0:T(8,128)(2,1)} %get-tuple-element.92) | copy-start | bytes 2359300
  469.1 30.9 %collective-permute-start.9 = (bf16[2,256,1536]{1,2,0:T(8,128)(2,1)}, bf16[2,256,1536]{1,2,0:T(8,128)(2,1)}, u32[]{:S(2)}, u32[]{:S(2)}) collective-permute-start(bf16[2,256,1536]{1,2,0:T(8,128)(2,1)} %fusion.52), channel_id=1, source_target_pairs={{1,0},{2,1},{3,2},{4,3},{5,4},{6,5},{7,6},{8,7},{9,8},{10,9},{11,1... | collective-permute-start | bytes 4718600 | tf_op jit(solution)/shard_map/ppermute | solution.py:17
  471.4 22.5 %collective-permute-start.4 = (bf16[15,1536]{0,1:T(8,128)(2,1)}, bf16[15,1536]{0,1:T(8,128)(2,1)S(1)}, u32[]{:S(2)}, u32[]{:S(2)}) collective-permute-start(bf16[15,1536]{0,1:T(8,128)(2,1)} %bitcast.9), channel_id=1, source_target_pairs={{0,1},{1,2},{2,3},{3,4},{4,5},{5,6},{6,7},{7,8},{8,9},{9,10},{10,1... | collective-permute-start | bytes 138248 | tf_op jit(solution)/shard_map/ppermute | solution.py:25
  492.6 11.7 %collective-permute-start.5 = (bf16[15,1536]{0,1:T(8,128)(2,1)S(1)}, bf16[15,1536]{0,1:T(8,128)(2,1)S(1)}, u32[]{:S(2)}, u32[]{:S(2)}) collective-permute-start(bf16[15,1536]{0,1:T(8,128)(2,1)S(1)} %bitcast.187), channel_id=1, source_target_pairs={{1,0},{2,1},{3,2},{4,3},{5,4},{6,5},{7,6},{8,7},{9,8},{10,9},{11,1... | collective-permute-start | bytes 138248 | tf_op jit(solution)/shard_map/ppermute | solution.py:28
  493.9 34.5 %slice-start.2 = ((s8[7864320]{0:T(1024)(128)(4,1)}), s8[4194304]{0:T(1024)(128)(4,1)S(1)}, s32[]{:S(2)}) async-start(s8[7864320]{0:T(1024)(128)(4,1)} %bitcast.160), calls=%async_computation.3 | async-start | bytes 8388608
  493.9 34.5 %slice-start.4 = ((s8[7864320]{0:T(1024)(128)(4,1)}), s8[4194304]{0:T(1024)(128)(4,1)S(1)}, s32[]{:S(2)}) async-start(s8[7864320]{0:T(1024)(128)(4,1)} %bitcast.167), calls=%async_computation.5 | async-start | bytes 8388608
  499.6 4.7 copy-start.7
  499.6 4.7 copy-start.8
  499.6 4.7 copy-start.9
  499.7 4.7 copy-start.10
  499.7 4.7 copy-start.11
  499.7 4.7 copy-start.12
  499.7 4.7 copy-start.13
  499.7 4.7 copy-start.14
  499.7 4.7 copy-start.15
  499.7 4.7 copy-start.16
  499.7 4.7 copy-start.17
  499.7 4.7 copy-start.18
  499.7 4.7 copy-start.19
  499.8 4.7 copy-start.20
  499.8 4.7 copy-start.21
  499.8 4.7 copy-start.22
  499.8 4.7 copy-start.23
  499.8 4.7 copy-start.24
  499.8 4.7 copy-start.25
  499.8 4.7 copy-start.26
  499.8 4.7 copy-start.27
  499.8 4.7 copy-start.28
  499.8 4.7 copy-start.29
  499.9 28.5 %slice-start.3 = ((s8[7864320]{0:T(1024)(128)(4,1)}), s8[3670016]{0:T(1024)(128)(4,1)S(1)}, s32[]{:S(2)}) async-start(s8[7864320]{0:T(1024)(128)(4,1)} %bitcast.160), calls=%async_computation.4 | async-start | bytes 7340032
  499.9 28.5 %slice-start.5 = ((s8[7864320]{0:T(1024)(128)(4,1)}), s8[3670016]{0:T(1024)(128)(4,1)S(1)}, s32[]{:S(2)}) async-start(s8[7864320]{0:T(1024)(128)(4,1)} %bitcast.167), calls=%async_computation.6 | async-start | bytes 7340032
  502.9 25.6 %collective-permute-start.10 = (bf16[2,256,1536]{1,2,0:T(8,128)(2,1)S(1)}, bf16[2,256,1536]{1,2,0:T(8,128)(2,1)S(1)}, u32[]{:S(2)}, u32[]{:S(2)}) collective-permute-start(bf16[2,256,1536]{1,2,0:T(8,128)(2,1)S(1)} %fusion.55), channel_id=1, source_target_pairs={{1,0},{2,1},{3,2},{4,3},{5,4},{6,5},{7,6},{8,7},{9,8},{10,9},{11,1... | collective-permute-start | bytes 4718600 | tf_op jit(solution)/shard_map/ppermute | solution.py:17
  530.1 22.7 %collective-permute-start.11 = (bf16[2,256,1536]{1,2,0:T(8,128)(2,1)}, bf16[2,256,1536]{1,2,0:T(8,128)(2,1)}, u32[]{:S(2)}, u32[]{:S(2)}) collective-permute-start(bf16[2,256,1536]{1,2,0:T(8,128)(2,1)} %fusion.47), channel_id=1, source_target_pairs={{1,0},{2,1},{3,2},{4,3},{5,4},{6,5},{7,6},{8,7},{9,8},{10,9},{11,1... | collective-permute-start | bytes 4718600 | tf_op jit(solution)/shard_map/ppermute | solution.py:17
  (9 other events, 35.4 us)
Sparse Core Ops, SparseCore 0:
  549.9 120.8 all-reduce.1
where the time goes:
time: 686 us; the launch traced here: 679 us
  matrix products  272 us (40%)
  waiting for transfers between devices  131 us (19%)
  other arithmetic  99.1 us (14%)
  starting transfers between devices  85.1 us (12%)
  local copies, waits for them, and re-layouts  76.1 us (11%)
  between operations  15.2 us (2%)
    psum x1, waiting for transfers between devices, local(): kernel_grad = lax.psum(jnp.stack(taps_grad), 'seq')  113 us
    dot_general x48, matrix products, attend(): jnp.dot(query_head, key_head.T, preferred_element_type=jnp.float32) * SCALE  69 us
    ppermute x8, starting transfers between devices, shifted(): return lax.ppermute(block, axis, route)  59.1 us
    dot_general x24, matrix products, forward_head(): jnp.dot(probs.astype(jnp.bfloat16), value_head, preferred_element_type=jn...  49.4 us
    dot_general x24, matrix products, backward_head(): jnp.dot(scores_grad, key_head, preferred_element_type=jnp.float32)  46.7 us
    dot_general x24, matrix products, backward_head(): jnp.einsum('qk,qd->kd', probs_half, grad_head, preferred_element_type=jnp...  45.8 us
    dot_general x24, matrix products, backward_head(): jnp.dot(grad_head, value_head.T, preferred_element_type=jnp.float32)  36.4 us
    unnamed x106, local copies, waits for them, and re-layouts  34.1 us
  transfers between devices with their start and end apart: 13, of which 6 were waited for; matrix products, arithmetic and copies ran while one was open for 14% of the time, Pallas kernels for 0%

commit v1 on v0

--- a/solution.py
+++ b/solution.py
@@ -9,6 +9,11 @@
 SPAN_DEV = 4
 SCALE = 0.125
 NEG = -1e30
+
+
+def store_the_samples(message, axis_id):
+    piece_now = lax.all_gather(message, axis_name=axis_id)
+    return jnp.sum(piece_now, 0)
 
 
 def shifted(block, axis, distance):
@@ -100,7 +105,7 @@
         taps_grad.append(jnp.sum(cot_float * window, axis=0))
     conv_out = conv_sum.astype(jnp.bfloat16)
     attended_grad = grad_sum.astype(jnp.bfloat16)
-    kernel_grad = lax.psum(jnp.stack(taps_grad), "seq")
+    kernel_grad = store_the_samples(jnp.stack(taps_grad), "seq")
     grad_heads = head_major(attended_grad, heads)
     out_heads = head_major(attended, heads)
     deltas = jnp.sum(grad_heads.astype(jnp.float32) * out_heads, axis=-1)

time: 686 us -> 624 us (0.910)
  the two profiles are of different devices: /device:TPU:0 before, /device:TPU:25 now
where the time goes in v1:
time: 624 us; the launch traced here: 617 us
  matrix products  272 us (44%)
  waiting for transfers between devices  115 us (18%)
  other arithmetic  105 us (17%)
  local copies, waits for them, and re-layouts  73.7 us (12%)
  starting transfers between devices  35.1 us (6%)
  between operations  15.1 us (2%)
    ppermute x8, waiting for transfers between devices, shifted(): return lax.ppermute(block, axis, route)  74.6 us
    dot_general x48, matrix products, attend(): jnp.dot(query_head, key_head.T, preferred_element_type=jnp.float32) * SCALE  69 us
    dot_general x24, matrix products, forward_head(): jnp.dot(probs.astype(jnp.bfloat16), value_head, preferred_element_type=jn...  49.4 us
    dot_general x24, matrix products, backward_head(): jnp.dot(scores_grad, key_head, preferred_element_type=jnp.float32)  46.7 us
    dot_general x24, matrix products, backward_head(): jnp.einsum('qk,qd->kd', probs_half, grad_head, preferred_element_type=jnp...  45.8 us
    ppermute x2, waiting for transfers between devices, with_halo(): lax.ppermute(lax.slice_in_dim(block, 0, width, axis=dim), axis, backward)  38.2 us
    dot_general x24, matrix products, backward_head(): jnp.dot(grad_head, value_head.T, preferred_element_type=jnp.float32)  36.4 us
    unnamed x95, local copies, waits for them, and re-layouts  32.5 us
  transfers between devices with their start and end apart: 13, of which 8 were waited for; matrix products, arithmetic and copies ran while one was open for 16% of the time, Pallas kernels for 0%

profile of v1, /device:TPU:25, one launch (start us, length us, event | category | flops | bytes accessed | tf_op | source)
XLA Modules:
  0.0 617.1 jit_solution(13016545467127315480)
XLA Ops:
  10.4 3.7 collective-permute-start
  14.2 17.3 %collective-permute-done = bf16[2,256,1536]{1,2,0:T(8,128)(2,1)S(1)} collective-permute-done((bf16[2,256,1536]{1,2,0:T(8,128)(2,1)S(1)}, bf16[2,256,1536]{1,2,0:T(8,128)(2,1)S(1)}, u32[]{:S(2)}, u32[]{:S(2)}) %collective-permute-start) | collective-permute-done | bytes 1572896 | tf_op jit(solution)/shard_map/ppermute | solution.py:22
  32.6 4.4 collective-permute-start.1
  37.0 17.3 %collective-permute-done.1 = bf16[2,256,1536]{1,2,0:T(8,128)(2,1)} collective-permute-done((bf16[2,256,1536]{1,2,0:T(8,128)(2,1)S(1)}, bf16[2,256,1536]{1,2,0:T(8,128)(2,1)}, u32[]{:S(2)}, u32[]{:S(2)}) %collective-permute-start.1) | collective-permute-done | bytes 1572896 | tf_op jit(solution)/shard_map/ppermute | solution.py:22
  54.4 4.5 collective-permute-start.2
  62.7 2.6 collective-permute-start.6
  65.7 2.1 slice_reduce_fusion.29
  67.8 2.5 slice_reduce_fusion.30
  72.8 3.7 collective-permute-done.2
  76.5 4.4 collective-permute-start.3
  80.9 24.2 %collective-permute-done.6 = bf16[15,1536]{0,1:T(8,128)(2,1)} collective-permute-done((bf16[15,1536]{0,1:T(8,128)(2,1)}, bf16[15,1536]{0,1:T(8,128)(2,1)}, u32[]{:S(2)}, u32[]{:S(2)}) %collective-permute-start.6) | collective-permute-done | bytes 46112 | tf_op jit(solution)/shard_map/ppermute | solution.py:33
  105.2 27.4 %fusion.136 = bf16[256,1536]{0,1:T(8,128)(2,1)} fusion(bf16[256,1536]{0,1:T(8,128)(2,1)S(1)} %copy.92, bf16[15,1536]{0,1:T(8,128)(2,1)S(1)} %collective-permute-done.7, bf16[15,1536]{0,1:T(8,128)(2,1)} %collective-permute-done.6, f32[1536]{0:T(1024)} %get-tuple-element.277, f32[1536]{0:T(1024)} %get-tuple-element.278, f32[1536]{0:T(1024)} %get-tuple-element.249, ...), kind=kLoop, calls=%fused_computation.330 | loop fusion | flops 71958528 | bytes 1855488 | tf_op jit(solution)/shard_map/convert_element_type | solution.py:107
  133.9 2.7 constant_dynamic-update-slice_fusion.2
  136.6 2.8 constant_dynamic-update-slice_fusion.1
  140.7 5.6 fusion.195
  146.3 8.3 %copy.89 = bf16[24,1280,64]{2,1,0:T(8,128)(2,1)} copy(bf16[24,1280,64]{1,2,0:T(8,128)(2,1)} %bitcast.174) | data formatting | bytes 7864320
  154.5 8.2 %copy.90 = bf16[24,1280,64]{2,1,0:T(8,128)(2,1)} copy(bf16[24,1280,64]{1,2,0:T(8,128)(2,1)} %bitcast.173) | data formatting | bytes 7864320
  162.8 104.6 %while.28 = (s32[]{:T(128)}, f32[24,256,64]{1,2,0:T(8,128)}, bf16[24,256,64]{2,1,0:T(8,128)(2,1)S(1)}, bf16[24,1280,64]{2,1,0:T(8,128)(2,1)}, bf16[24,1280,64]{2,1,0:T(8,128)(2,1)}, /*index=5*/pred[256,10]{0,1:T(8,128)(4,1)S(1)}) while((s32[]{:T(128)}, f32[24,256,64]{1,2,0:T(8,128)}, ...), condition=%wide.region_4.5_spmd.clone.clone, body=%wide.region_1.4_spmd.clone.sunk.clone | while | flops 86507008 | bytes 6039117 | solution.py:90
  178.1 2.1 fusion.239
  191.2 2.1 fusion.239
  204.3 2.1 fusion.239
  208.6 2.1 fusion.239
  217.4 2.1 fusion.239
  221.7 2.1 fusion.239
  243.5 2.1 fusion.239
  247.9 2.1 fusion.239
  252.2 2.1 fusion.239
  265.3 2.1 fusion.239
  267.4 2.5 multiply_reduce_fusion
  269.9 208.7 %while.29 = (s32[]{:T(128)}, bf16[24,256,64]{1,2,0:T(8,128)(2,1)}, f32[24,1280,64]{1,2,0:T(8,128)}, f32[24,1280,64]{1,2,0:T(8,128)}, bf16[24,256,64]{2,1,0:T(8,1...) while((s32[]{:T(128)}, bf16[24,256,64]{1,2,0:T(8,128)(2,1)}, ...), condition=%wide.region_9.10_spmd.clone.clone, body=%wide.region_6.9_spmd.clone.sunk.clone | while | flops 214302208 | bytes 10438257 | solution.py:128
  478.6 2.3 fusion.49
  480.9 2.3 collective-permute-start.8
  483.4 3.5 collective-permute-start.4
  487.0 2.1 collective-permute-start.5
  489.1 2.6 collective-permute-done.4
  491.7 5.6 fusion.119
  497.3 14.0 %collective-permute-done.5 = bf16[15,1536]{0,1:T(8,128)(2,1)S(1)} collective-permute-done((bf16[15,1536]{0,1:T(8,128)(2,1)S(1)}, bf16[15,1536]{0,1:T(8,128)(2,1)S(1)}, u32[]{:S(2)}, u32[]{:S(2)}) %collective-permute-start.5) | collective-permute-done | bytes 46112 | tf_op jit(solution)/shard_map/ppermute | solution.py:33
  511.3 6.0 fusion.135
  520.8 3.7 fusion.118
  524.7 4.4 fusion.134
  529.3 2.8 stack.143
  532.1 8.9 %collective-permute-done.9 = bf16[2,256,1536]{1,2,0:T(8,128)(2,1)} collective-permute-done((bf16[2,256,1536]{1,2,0:T(8,128)(2,1)}, bf16[2,256,1536]{1,2,0:T(8,128)(2,1)}, u32[]{:S(2)}, u32[]{:S(2)}) %collective-permute-start.9) | collective-permute-done | bytes 1572896 | tf_op jit(solution)/shard_map/ppermute | solution.py:22
  541.0 4.0 fusion.55
  548.3 27.4 %collective-permute-done.10 = bf16[2,256,1536]{1,2,0:T(8,128)(2,1)} collective-permute-done((bf16[2,256,1536]{1,2,0:T(8,128)(2,1)}, bf16[2,256,1536]{1,2,0:T(8,128)(2,1)}, u32[]{:S(2)}, u32[]{:S(2)}) %collective-permute-start.10) | collective-permute-done | bytes 1572896 | tf_op jit(solution)/shard_map/ppermute | solution.py:22
  575.7 4.0 fusion.47
  581.9 19.3 %fusion.88 = bf16[256,1536]{0,1:T(8,128)(2,1)S(1)} fusion(bf16[256,1536]{0,1:T(8,128)(2,1)S(1)} %bitcast.170, f32[1536]{0:T(1024)S(1)} %copy-done.36, f32[1536]{0:T(1024)S(1)} %copy-done.37, f32[1536]{0:T(1024)S(1)} %copy-done.8, f32[1536]{0:T(1024)S(1)} %copy-done.9, f32[1536]{0:T(1024)S(1)} %copy-done.10, f32[1536]{0:T(1024)S(1)} %copy-done.11, ...), kind=kLoop, calls=%fused_computation.280 | loop fusion | flops 71958528 | bytes 1855488 | tf_op jit(solution)/shard_map/convert_element_type | solution.py:106
  602.4 2.8 reduce_sum.347
  605.1 2.7 fusion.57
  (479 shorter events, 318.2 us)
Async XLA Ops:
  7.2 595.2 %all-gather.4.cloned.1.call-start = ((), (), s32[]{:S(2)}) async-start(), calls=%async_computation | async-start | bytes 3342336 | tf_op jit(solution)/shard_map/all_gather | solution.py:15
  9.0 49.9 %copy-start.5 = (bf16[256,1536]{1,0:T(8,128)(2,1)S(1)}, bf16[256,1536]{1,0:T(8,128)(2,1)}, u32[]{:S(2)}) copy-start(bf16[256,1536]{1,0:T(8,128)(2,1)} %param.15) | copy-start | bytes 2359300
  9.0 56.5 %copy-start.38 = (s32[2,4]{1,0:T(2,128)S(1)}, s32[2,4]{1,0:T(2,128)}, u32[]{:S(2)}) copy-start(s32[2,4]{1,0:T(2,128)} %param.13) | copy-start | bytes 100
  10.4 21.0 %collective-permute-start = (bf16[2,256,1536]{1,2,0:T(8,128)(2,1)S(1)}, bf16[2,256,1536]{1,2,0:T(8,128)(2,1)S(1)}, u32[]{:S(2)}, u32[]{:S(2)}) collective-permute-start(bf16[2,256,1536]{1,2,0:T(8,128)(2,1)S(1)} %get-tuple-element.321), channel_id=1, source_target_pairs={{0,1},{1,2},{2,3},{3,4},{4,5},{5,6},{6,7},{7,8},{8,9},{9,10},{10,1... | collective-permute-start | bytes 4718600 | tf_op jit(solution)/shard_map/ppermute | solution.py:22
  32.6 21.7 %collective-permute-start.1 = (bf16[2,256,1536]{1,2,0:T(8,128)(2,1)S(1)}, bf16[2,256,1536]{1,2,0:T(8,128)(2,1)}, u32[]{:S(2)}, u32[]{:S(2)}) collective-permute-start(bf16[2,256,1536]{1,2,0:T(8,128)(2,1)S(1)} %collective-permute-done), channel_id=1, source_target_pairs={{0,1},{1,2},{2,3},{3,4},{4,5},{5,6},{6,7},{7,8},{8,9},{9,10},{10,1... | collective-permute-start | bytes 4718600 | tf_op jit(solution)/shard_map/ppermute | solution.py:22
  54.4 22.1 %collective-permute-start.2 = (bf16[2,256,1536]{1,2,0:T(8,128)(2,1)}, bf16[2,256,1536]{1,2,0:T(8,128)(2,1)}, u32[]{:S(2)}, u32[]{:S(2)}) collective-permute-start(bf16[2,256,1536]{1,2,0:T(8,128)(2,1)} %collective-permute-done.1), channel_id=1, source_target_pairs={{0,1},{1,2},{2,3},{3,4},{4,5},{5,6},{6,7},{7,8},{8,9},{9,10},{10,1... | collective-permute-start | bytes 4718600 | tf_op jit(solution)/shard_map/ppermute | solution.py:22
  59.8 21.0 %collective-permute-start.7 = (bf16[15,1536]{0,1:T(8,128)(2,1)}, bf16[15,1536]{0,1:T(8,128)(2,1)S(1)}, u32[]{:S(2)}, u32[]{:S(2)}) collective-permute-start(bf16[15,1536]{0,1:T(8,128)(2,1)} %copy.94), channel_id=1, source_target_pairs={{0,1},{1,2},{2,3},{3,4},{4,5},{5,6},{6,7},{7,8},{8,9},{9,10},{10,1... | collective-permute-start | bytes 138248 | tf_op jit(solution)/shard_map/ppermute | solution.py:30
  62.7 42.4 %collective-permute-start.6 = (bf16[15,1536]{0,1:T(8,128)(2,1)}, bf16[15,1536]{0,1:T(8,128)(2,1)}, u32[]{:S(2)}, u32[]{:S(2)}) collective-permute-start(bf16[15,1536]{0,1:T(8,128)(2,1)} %copy.91), channel_id=1, source_target_pairs={{1,0},{2,1},{3,2},{4,3},{5,4},{6,5},{7,6},{8,7},{9,8},{10,9},{11,1... | collective-permute-start | bytes 138248 | tf_op jit(solution)/shard_map/ppermute | solution.py:33
  72.8 59.7 %copy-start.4 = (bf16[2,256,1536]{1,2,0:T(8,128)(2,1)S(1)}, bf16[2,256,1536]{1,2,0:T(8,128)(2,1)}, u32[]{:S(2)}) copy-start(bf16[2,256,1536]{1,2,0:T(8,128)(2,1)} %copy-done.3) | copy-start | bytes 4718596
  76.5 62.9 %collective-permute-start.3 = (bf16[2,256,1536]{1,2,0:T(8,128)(2,1)}, bf16[2,256,1536]{1,2,0:T(8,128)(2,1)S(1)}, u32[]{:S(2)}, u32[]{:S(2)}) collective-permute-start(bf16[2,256,1536]{1,2,0:T(8,128)(2,1)} %collective-permute-done.2), channel_id=1, source_target_pairs={{0,1},{1,2},{2,3},{3,4},{4,5},{5,6},{6,7},{7,8},{8,9},{9,10},{10,1... | collective-permute-start | bytes 4718600 | tf_op jit(solution)/shard_map/ppermute | solution.py:22
  478.6 38.7 %copy-start = (f32[24,1280,64]{1,2,0:T(8,128)S(1)}, f32[24,1280,64]{1,2,0:T(8,128)}, u32[]{:S(2)}) copy-start(f32[24,1280,64]{1,2,0:T(8,128)} %get-tuple-element.94) | copy-start | bytes 23592964
  478.6 38.7 %copy-start.1 = (f32[24,1280,64]{1,2,0:T(8,128)S(1)}, f32[24,1280,64]{1,2,0:T(8,128)}, u32[]{:S(2)}) copy-start(f32[24,1280,64]{1,2,0:T(8,128)} %get-tuple-element.93) | copy-start | bytes 23592964
  480.9 36.4 %collective-permute-start.8 = (bf16[2,256,1536]{1,2,0:T(8,128)(2,1)S(1)}, bf16[2,256,1536]{1,2,0:T(8,128)(2,1)S(1)}, u32[]{:S(2)}, u32[]{:S(2)}) collective-permute-start(bf16[2,256,1536]{1,2,0:T(8,128)(2,1)S(1)} %fusion.49), channel_id=1, source_target_pairs={{1,0},{2,1},{3,2},{4,3},{5,4},{6,5},{7,6},{8,7},{9,8},{10,9},{11,1... | collective-permute-start | bytes 4718600 | tf_op jit(solution)/shard_map/ppermute | solution.py:22
  483.4 8.2 %collective-permute-start.4 = (bf16[15,1536]{0,1:T(8,128)(2,1)S(1)}, bf16[15,1536]{0,1:T(8,128)(2,1)S(1)}, u32[]{:S(2)}, u32[]{:S(2)}) collective-permute-start(bf16[15,1536]{0,1:T(8,128)(2,1)S(1)} %bitcast.184), channel_id=1, source_target_pairs={{0,1},{1,2},{2,3},{3,4},{4,5},{5,6},{6,7},{7,8},{8,9},{9,10},{10,1... | collective-permute-start | bytes 138248 | tf_op jit(solution)/shard_map/ppermute | solution.py:30
  487.0 24.3 %collective-permute-start.5 = (bf16[15,1536]{0,1:T(8,128)(2,1)S(1)}, bf16[15,1536]{0,1:T(8,128)(2,1)S(1)}, u32[]{:S(2)}, u32[]{:S(2)}) collective-permute-start(bf16[15,1536]{0,1:T(8,128)(2,1)S(1)} %bitcast.183), channel_id=1, source_target_pairs={{1,0},{2,1},{3,2},{4,3},{5,4},{6,5},{7,6},{8,7},{9,8},{10,9},{11,1... | collective-permute-start | bytes 138248 | tf_op jit(solution)/shard_map/ppermute | solution.py:33
  518.9 22.0 %collective-permute-start.9 = (bf16[2,256,1536]{1,2,0:T(8,128)(2,1)}, bf16[2,256,1536]{1,2,0:T(8,128)(2,1)}, u32[]{:S(2)}, u32[]{:S(2)}) collective-permute-start(bf16[2,256,1536]{1,2,0:T(8,128)(2,1)} %fusion.52), channel_id=1, source_target_pairs={{1,0},{2,1},{3,2},{4,3},{5,4},{6,5},{7,6},{8,7},{9,8},{10,9},{11,1... | collective-permute-start | bytes 4718600 | tf_op jit(solution)/shard_map/ppermute | solution.py:22
  545.0 30.8 %collective-permute-start.10 = (bf16[2,256,1536]{1,2,0:T(8,128)(2,1)}, bf16[2,256,1536]{1,2,0:T(8,128)(2,1)}, u32[]{:S(2)}, u32[]{:S(2)}) collective-permute-start(bf16[2,256,1536]{1,2,0:T(8,128)(2,1)} %fusion.55), channel_id=1, source_target_pairs={{1,0},{2,1},{3,2},{4,3},{5,4},{6,5},{7,6},{8,7},{9,8},{10,9},{11,1... | collective-permute-start | bytes 4718600 | tf_op jit(solution)/shard_map/ppermute | solution.py:22
  548.1 33.6 %copy-start.8 = (f32[1536]{0:T(1024)S(1)}, f32[1536]{0:T(1024)}, u32[]{:S(2)}) copy-start(f32[1536]{0:T(1024)} %get-tuple-element.249) | copy-start | bytes 18436
  548.1 33.6 %copy-start.9 = (f32[1536]{0:T(1024)S(1)}, f32[1536]{0:T(1024)}, u32[]{:S(2)}) copy-start(f32[1536]{0:T(1024)} %get-tuple-element.250) | copy-start | bytes 18436
  548.1 33.6 %copy-start.10 = (f32[1536]{0:T(1024)S(1)}, f32[1536]{0:T(1024)}, u32[]{:S(2)}) copy-start(f32[1536]{0:T(1024)} %get-tuple-element.251) | copy-start | bytes 18436
  548.1 33.6 %copy-start.11 = (f32[1536]{0:T(1024)S(1)}, f32[1536]{0:T(1024)}, u32[]{:S(2)}) copy-start(f32[1536]{0:T(1024)} %get-tuple-element.252) | copy-start | bytes 18436
  548.1 33.6 %copy-start.12 = (f32[1536]{0:T(1024)S(1)}, f32[1536]{0:T(1024)}, u32[]{:S(2)}) copy-start(f32[1536]{0:T(1024)} %get-tuple-element.253) | copy-start | bytes 18436
  548.1 33.6 %copy-start.13 = (f32[1536]{0:T(1024)S(1)}, f32[1536]{0:T(1024)}, u32[]{:S(2)}) copy-start(f32[1536]{0:T(1024)} %get-tuple-element.254) | copy-start | bytes 18436
  548.1 33.6 %copy-start.14 = (f32[1536]{0:T(1024)S(1)}, f32[1536]{0:T(1024)}, u32[]{:S(2)}) copy-start(f32[1536]{0:T(1024)} %get-tuple-element.255) | copy-start | bytes 18436
  548.1 33.6 %copy-start.15 = (f32[1536]{0:T(1024)S(1)}, f32[1536]{0:T(1024)}, u32[]{:S(2)}) copy-start(f32[1536]{0:T(1024)} %get-tuple-element.256) | copy-start | bytes 18436
  548.1 33.6 %copy-start.16 = (f32[1536]{0:T(1024)S(1)}, f32[1536]{0:T(1024)}, u32[]{:S(2)}) copy-start(f32[1536]{0:T(1024)} %get-tuple-element.257) | copy-start | bytes 18436
  548.1 33.6 %copy-start.17 = (f32[1536]{0:T(1024)S(1)}, f32[1536]{0:T(1024)}, u32[]{:S(2)}) copy-start(f32[1536]{0:T(1024)} %get-tuple-element.258) | copy-start | bytes 18436
  548.1 33.6 %copy-start.18 = (f32[1536]{0:T(1024)S(1)}, f32[1536]{0:T(1024)}, u32[]{:S(2)}) copy-start(f32[1536]{0:T(1024)} %get-tuple-element.259) | copy-start | bytes 18436
  548.1 33.6 %copy-start.19 = (f32[1536]{0:T(1024)S(1)}, f32[1536]{0:T(1024)}, u32[]{:S(2)}) copy-start(f32[1536]{0:T(1024)} %get-tuple-element.260) | copy-start | bytes 18436
  548.2 33.6 %copy-start.20 = (f32[1536]{0:T(1024)S(1)}, f32[1536]{0:T(1024)}, u32[]{:S(2)}) copy-start(f32[1536]{0:T(1024)} %get-tuple-element.261) | copy-start | bytes 18436
  548.2 33.6 %copy-start.21 = (f32[1536]{0:T(1024)S(1)}, f32[1536]{0:T(1024)}, u32[]{:S(2)}) copy-start(f32[1536]{0:T(1024)} %get-tuple-element.262) | copy-start | bytes 18436
  548.2 33.6 %copy-start.22 = (f32[1536]{0:T(1024)S(1)}, f32[1536]{0:T(1024)}, u32[]{:S(2)}) copy-start(f32[1536]{0:T(1024)} %get-tuple-element.263) | copy-start | bytes 18436
  548.2 33.6 %copy-start.23 = (f32[1536]{0:T(1024)S(1)}, f32[1536]{0:T(1024)}, u32[]{:S(2)}) copy-start(f32[1536]{0:T(1024)} %get-tuple-element.264) | copy-start | bytes 18436
  548.2 33.6 %copy-start.24 = (f32[1536]{0:T(1024)S(1)}, f32[1536]{0:T(1024)}, u32[]{:S(2)}) copy-start(f32[1536]{0:T(1024)} %get-tuple-element.265) | copy-start | bytes 18436
  548.2 33.6 %copy-start.25 = (f32[1536]{0:T(1024)S(1)}, f32[1536]{0:T(1024)}, u32[]{:S(2)}) copy-start(f32[1536]{0:T(1024)} %get-tuple-element.266) | copy-start | bytes 18436
  548.2 33.6 %copy-start.26 = (f32[1536]{0:T(1024)S(1)}, f32[1536]{0:T(1024)}, u32[]{:S(2)}) copy-start(f32[1536]{0:T(1024)} %get-tuple-element.267) | copy-start | bytes 18436
  548.2 33.6 %copy-start.27 = (f32[1536]{0:T(1024)S(1)}, f32[1536]{0:T(1024)}, u32[]{:S(2)}) copy-start(f32[1536]{0:T(1024)} %get-tuple-element.268) | copy-start | bytes 18436
  548.2 33.6 %copy-start.28 = (f32[1536]{0:T(1024)S(1)}, f32[1536]{0:T(1024)}, u32[]{:S(2)}) copy-start(f32[1536]{0:T(1024)} %get-tuple-element.269) | copy-start | bytes 18436
  548.3 33.6 %copy-start.29 = (f32[1536]{0:T(1024)S(1)}, f32[1536]{0:T(1024)}, u32[]{:S(2)}) copy-start(f32[1536]{0:T(1024)} %get-tuple-element.270) | copy-start | bytes 18436
  548.3 33.6 %copy-start.30 = (f32[1536]{0:T(1024)S(1)}, f32[1536]{0:T(1024)}, u32[]{:S(2)}) copy-start(f32[1536]{0:T(1024)} %get-tuple-element.271) | copy-start | bytes 18436
  548.3 33.6 %copy-start.31 = (f32[1536]{0:T(1024)S(1)}, f32[1536]{0:T(1024)}, u32[]{:S(2)}) copy-start(f32[1536]{0:T(1024)} %get-tuple-element.272) | copy-start | bytes 18436
  548.3 33.6 %copy-start.32 = (f32[1536]{0:T(1024)S(1)}, f32[1536]{0:T(1024)}, u32[]{:S(2)}) copy-start(f32[1536]{0:T(1024)} %get-tuple-element.273) | copy-start | bytes 18436
  548.3 33.6 %copy-start.33 = (f32[1536]{0:T(1024)S(1)}, f32[1536]{0:T(1024)}, u32[]{:S(2)}) copy-start(f32[1536]{0:T(1024)} %get-tuple-element.274) | copy-start | bytes 18436
  548.3 33.6 %copy-start.34 = (f32[1536]{0:T(1024)S(1)}, f32[1536]{0:T(1024)}, u32[]{:S(2)}) copy-start(f32[1536]{0:T(1024)} %get-tuple-element.275) | copy-start | bytes 18436
  548.3 33.6 %copy-start.35 = (f32[1536]{0:T(1024)S(1)}, f32[1536]{0:T(1024)}, u32[]{:S(2)}) copy-start(f32[1536]{0:T(1024)} %get-tuple-element.276) | copy-start | bytes 18436
  548.3 33.6 %copy-start.36 = (f32[1536]{0:T(1024)S(1)}, f32[1536]{0:T(1024)}, u32[]{:S(2)}) copy-start(f32[1536]{0:T(1024)} %get-tuple-element.277) | copy-start | bytes 18436
  548.3 33.6 %copy-start.37 = (f32[1536]{0:T(1024)S(1)}, f32[1536]{0:T(1024)}, u32[]{:S(2)}) copy-start(f32[1536]{0:T(1024)} %get-tuple-element.278) | copy-start | bytes 18436
  579.7 25.4 %collective-permute-start.11 = (bf16[2,256,1536]{1,2,0:T(8,128)(2,1)}, bf16[2,256,1536]{1,2,0:T(8,128)(2,1)}, u32[]{:S(2)}, u32[]{:S(2)}) collective-permute-start(bf16[2,256,1536]{1,2,0:T(8,128)(2,1)} %fusion.47), channel_id=1, source_target_pairs={{1,0},{2,1},{3,2},{4,3},{5,4},{6,5},{7,6},{8,7},{9,8},{10,9},{11,1... | collective-permute-start | bytes 4718600 | tf_op jit(solution)/shard_map/ppermute | solution.py:22
  (4 other events, 27.4 us)
Sparse Core Ops, SparseCore 0:
  532.2 49.1 all-gather.3
